TPU v7x, 32 devices: a whole 2x2x4 slice. The times are simulated.
32 devices in a mesh: grp: 2 (over y), ex: 4 (over z), feat: 4 (over x, core).
Axes of the slice: x: 2, y: 2, z: 4, core: 2. Of those that a mesh axis runs over, the one named last changes fastest.
Arguments:
- queries: bfloat16 [2048, 32768], P(('grp', 'ex'), 'feat'), parts along dimension 0, may hold values from -6 to 6
- grads: bfloat16 [512, 32768], P(('grp', 'ex'), 'feat'), parts along dimension 0, may hold values from -0.03125 to 0.03125
- example_ids: int32 [8, 64], P(('grp', 'ex')), parts along dimension 0, may hold values from 0 to 63, each once within a row
- layer_of_block: int32 [32], P('feat'), may hold values from 0 to 79
- rot_out: bfloat16 [80, 32, 32], replicated, may hold values from -1 to 1
- rot_in: bfloat16 [80, 32, 32], replicated, may hold values from -1 to 1
- eig_out: float32 [80, 32], replicated, may hold values from 0.3 to 3
- eig_in: float32 [80, 32], replicated, may hold values from 0.3 to 3
Outputs:
- scores: float32 [512, 1024], P(('grp', 'ex'), 'feat'), parts along dimension 0
There are 2 independent parts, one for each index of `grp`. A program takes and returns all parts, laid end to end along the dimension named above; an argument that names none is the same for every part. Nothing has to cross between parts.
Inputs may be any that keep to these rules, and one draw needn't show every extreme that they name: Each row of example_ids holds every number of 0 to 63 once.
All inputs are finite; a program needn't handle non-finite values.
Results may differ from a plain program's by a relative error of at most 0.0048.
Values may be sent and summed in bfloat16 or wider, within the bound.
A program may use at most 64 MiB of HBM per device.

v0:
```python
import jax
import jax.numpy as jnp
from jax import lax
from jax.sharding import PartitionSpec as P

STEPS = 3


DAMPING = 0.1


def shifted(value, axis, steps):
    count = lax.axis_size(axis)
    pairs = [(source, (source + steps) % count) for source in range(count)]
    return lax.ppermute(value, axis, pairs)


def select_tables(layer_of_block, rot_out, rot_in, eig_out, eig_in):
    levels = jnp.arange(rot_out.shape[0], dtype=jnp.int32)
    onehot = layer_of_block[:, None] == levels[None, :]
    onehot_low = onehot.astype(jnp.bfloat16)
    onehot_full = onehot.astype(jnp.float32)
    out_basis = jnp.einsum(
        "bl,lpo->bpo", onehot_low, rot_out, preferred_element_type=jnp.float32
    ).astype(jnp.bfloat16)
    in_basis = jnp.einsum(
        "bl,lij->bij", onehot_low, rot_in, preferred_element_type=jnp.float32
    ).astype(jnp.bfloat16)
    out_vals = jnp.dot(onehot_full, eig_out, precision=lax.Precision.HIGHEST)
    in_vals = jnp.dot(onehot_full, eig_in, precision=lax.Precision.HIGHEST)
    inverse = 1.0 / (out_vals[:, :, None] * in_vals[:, None, :] + DAMPING)
    return (out_basis, in_basis, inverse)


def precondition(query_rows, out_basis, in_basis, inverse):
    rows = query_rows.shape[0]
    blocks = out_basis.shape[0]
    kout = out_basis.shape[1]
    kin = in_basis.shape[1]
    query_grid = query_rows.reshape(rows, blocks, kout, kin)
    first_rot = jnp.einsum(
        "bpo,nbpi->boin", out_basis, query_grid, preferred_element_type=jnp.float32
    ).astype(jnp.bfloat16)
    second_rot = (
        jnp.einsum("boin,bij->bojn", first_rot, in_basis, preferred_element_type=jnp.float32)
        * inverse[:, :, :, None]
    ).astype(jnp.bfloat16)
    third_rot = jnp.einsum(
        "bpo,bojn->bpjn", out_basis, second_rot, preferred_element_type=jnp.float32
    ).astype(jnp.bfloat16)
    ready = jnp.einsum(
        "bpjn,bij->nbpi", third_rot, in_basis, preferred_element_type=jnp.float32
    ).astype(jnp.bfloat16)
    return ready.reshape(rows, blocks * kout * kin)


def against(query_rows, grads):
    return lax.dot_general(
        query_rows, grads, (((1,), (1,)), ((), ())), preferred_element_type=jnp.float32
    )


def local(queries, grads, example_ids, layer_of_block, rot_out, rot_in, eig_out, eig_in):
    out_basis, in_basis, inverse = select_tables(layer_of_block, rot_out, rot_in, eig_out, eig_in)
    ready = precondition(queries, out_basis, in_basis, inverse)
    received = [ready]
    current = ready
    for offset in range(STEPS):
        current = shifted(current, "ex", 1)
        received.append(current)
    stacked = jnp.concatenate(received, axis=0)
    partial_value = against(stacked, grads)
    owned_rows = lax.psum_scatter(partial_value, "feat", scatter_dimension=0, tiled=True)
    example_major = owned_rows.T
    return jnp.take(example_major, example_ids[0], axis=0)


def solution(mesh):
    in_specs = (
        P(("grp", "ex"), "feat"),
        P(("grp", "ex"), "feat"),
        P(("grp", "ex"), None),
        P("feat"),
        P(),
        P(),
        P(),
        P(),
    )
    out_specs = P(("grp", "ex"), "feat")
    return jax.shard_map(local, mesh=mesh, in_specs=in_specs, out_specs=out_specs, check_vma=False)
```

profile of v0, /device:TPU:1, one launch (start us, length us, event | category | flops | bytes accessed | tf_op | source)
XLA Modules:
  0.0 353.0 jit_solution(6346232508664818461)
XLA Ops:
  6.5 0.0 copy-start
  6.5 0.0 copy-start.4
  6.5 0.0 copy-start.2
  6.5 0.0 copy-start.3
  6.5 0.0 copy-start.7
  6.5 0.0 copy-start.8
  6.6 0.0 reduce-scatter.2.cloned.1.call-start
  6.6 6.5 %copy.12 = bf16[256,8192]{0,1:T(8,128)(2,1)} copy(bf16[256,8192]{1,0:T(8,128)(2,1)} %param.8) | data formatting | bytes 8388608 | tf_op args[0]
  13.1 0.0 copy-done.4
  13.1 0.0 copy-done.2
  13.1 0.5 fusion.28
  13.5 0.0 copy-done.3
  13.5 0.5 fusion.27
  14.0 0.0 copy-done.7
  14.0 0.2 fusion.33
  14.2 0.0 copy-done.8
  14.2 0.2 fusion.34
  14.4 4.8 %convert_bitcast_fusion = bf16[8,32,32,256]{3,1,2,0:T(8,128)(2,1)S(1)} fusion(bf16[256,8,32,32]{0,3,2,1:T(8,128)(2,1)} %bitcast.32, bf16[8,32,32,1]{2,0,1,3:T(8,128)(2,1)S(1)} %fusion.28), kind=kOutput, calls=%fused_computation.19 | convolution fusion | flops 136314880 | bytes 8404992 | tf_op jit(solution)/shard_map/bpo,nbpi->boin/dot_general | solution.py:41
  19.2 0.1 add_divide_fusion
  19.3 6.4 %fusion.8 = bf16[8,32,32,256]{3,2,1,0:T(8,128)(2,1)S(1)} fusion(f32[8,32,32]{2,1,0:T(8,128)S(1)} %add_divide_fusion, bf16[8,32,32,256]{3,1,2,0:T(8,128)(2,1)S(1)} %convert_bitcast_fusion, bf16[8,32,32,1]{2,0,1,3:T(8,128)(2,1)S(1)} %fusion.27), kind=kOutput, calls=%fused_computation.10 | convolution fusion | flops 138412032 | bytes 8437760 | tf_op jit(solution)/shard_map/boin,bij->bojn/dot_general | solution.py:45
  25.7 2.5 fusion.19
  28.2 2.5 fusion.22
  30.8 0.0 copy-start.1
  30.8 1.9 copy-done.1
  32.7 0.0 copy-start.9
  32.7 2.1 collective-permute-start
  34.9 92.3 %collective-permute-done = bf16[256,8192]{0,1:T(8,128)(2,1)S(1)} collective-permute-done((bf16[256,8192]{0,1:T(8,128)(2,1)S(1)}, bf16[256,8192]{0,1:T(8,128)(2,1)S(1)}, u32[]{:S(2)}, u32[]{:S(2)}) %collective-permute-start) | collective-permute-done | bytes 4194336 | tf_op jit(solution)/shard_map/ppermute | solution.py:15
  127.2 0.0 copy-start.5
  127.2 2.0 copy-done.5
  129.1 0.0 collective-permute-start.1
  129.1 92.6 %collective-permute-done.1 = bf16[256,8192]{0,1:T(8,128)(2,1)S(1)} collective-permute-done((bf16[256,8192]{0,1:T(8,128)(2,1)S(1)}, bf16[256,8192]{0,1:T(8,128)(2,1)S(1)}, u32[]{:S(2)}, u32[]{:S(2)}) %collective-permute-start.1) | collective-permute-done | bytes 4194336 | tf_op jit(solution)/shard_map/ppermute | solution.py:15
  221.8 0.0 copy-start.6
  221.8 2.0 copy-done.6
  223.7 0.0 collective-permute-start.2
  223.7 91.8 %collective-permute-done.2 = bf16[256,8192]{0,1:T(8,128)(2,1)} collective-permute-done((bf16[256,8192]{0,1:T(8,128)(2,1)S(1)}, bf16[256,8192]{0,1:T(8,128)(2,1)}, u32[]{:S(2)}, u32[]{:S(2)}) %collective-permute-start.2) | collective-permute-done | bytes 4194336 | tf_op jit(solution)/shard_map/ppermute | solution.py:15
  315.6 0.0 copy-done
  315.6 8.1 %fusion = f32[1024,64]{0,1:T(8,128)} fusion(bf16[64,8192]{1,0:T(8,128)(2,1)S(1)} %copy-done, bf16[256,8192]{0,1:T(8,128)(2,1)} %collective-permute-done.2, bf16[256,8192]{0,1:T(8,128)(2,1)} %copy-done.6, bf16[256,8192]{0,1:T(8,128)(2,1)} %copy-done.5, bf16[256,8192]{0,1:T(8,128)(2,1)} %bitcast.34), kind=kOutput, calls=%fused_computation.1 | convolution fusion | flops 1140850688 | bytes 18087936 | tf_op jit(solution)/shard_map/dot_general | solution.py:58
  323.7 0.0 reduce-scatter.2.cloned.1.call-update
  323.7 0.0 copy-done.9
  323.7 20.2 %reduce-scatter.2.cloned.1.call-done = f32[256,64]{0,1:T(8,128)} async-done(((f32[1024,64]{0,1:T(8,128)}), f32[256,64]{0,1:T(8,128)}) %reduce-scatter.2.cloned.1.call-update) | async-done | bytes 65552 | tf_op jit(solution)/shard_map/reduce_scatter | solution.py:73
  343.9 1.5 gather_fusion
  345.4 0.7 broadcast_select_fusion
  (3 shorter events, 0.0 us)
Async XLA Ops:
  6.5 309.0 %copy-start = (bf16[64,8192]{1,0:T(8,128)(2,1)S(1)}, bf16[64,8192]{1,0:T(8,128)(2,1)}, u32[]{:S(2)}) copy-start(bf16[64,8192]{1,0:T(8,128)(2,1)} %param.9) | copy-start | bytes 3145732
  6.5 6.6 %copy-start.4 = (s32[8]{0:T(128)S(1)}, s32[8]{0:T(128)}, u32[]{:S(2)}) copy-start(s32[8]{0:T(128)} %param.11) | copy-start | bytes 100
  6.5 6.6 %copy-start.2 = (bf16[80,32,32]{0,2,1:T(8,128)(2,1)S(1)}, bf16[80,32,32]{0,2,1:T(8,128)(2,1)}, u32[]{:S(2)}) copy-start(bf16[80,32,32]{0,2,1:T(8,128)(2,1)} %param.12) | copy-start | bytes 491524
  6.5 7.0 %copy-start.3 = (bf16[80,32,32]{0,2,1:T(8,128)(2,1)S(1)}, bf16[80,32,32]{0,2,1:T(8,128)(2,1)}, u32[]{:S(2)}) copy-start(bf16[80,32,32]{0,2,1:T(8,128)(2,1)} %param.13) | copy-start | bytes 491524
  6.5 7.5 %copy-start.7 = (f32[80,32]{0,1:T(8,128)S(1)}, f32[80,32]{0,1:T(8,128)}, u32[]{:S(2)}) copy-start(f32[80,32]{0,1:T(8,128)} %param.14) | copy-start | bytes 30724
  6.5 7.7 %copy-start.8 = (f32[80,32]{0,1:T(8,128)S(1)}, f32[80,32]{0,1:T(8,128)}, u32[]{:S(2)}) copy-start(f32[80,32]{0,1:T(8,128)} %param.15) | copy-start | bytes 30724
  6.6 337.4 %reduce-scatter.2.cloned.1.call-start = ((), (), s32[]{:S(2)}) async-start(), calls=%async_computation.1 | async-start | bytes 327680 | tf_op jit(solution)/shard_map/reduce_scatter | solution.py:73
  30.8 1.9 copy-start.1
  32.7 291.0 %copy-start.9 = (s32[1,64]{1,0:T(1,128)S(1)}, s32[1,64]{1,0:T(1,128)}, u32[]{:S(2)}) copy-start(s32[1,64]{1,0:T(1,128)} %param.10) | copy-start | bytes 772
  32.7 94.4 %collective-permute-start = (bf16[256,8192]{0,1:T(8,128)(2,1)S(1)}, bf16[256,8192]{0,1:T(8,128)(2,1)S(1)}, u32[]{:S(2)}, u32[]{:S(2)}) collective-permute-start(bf16[256,8192]{0,1:T(8,128)(2,1)S(1)} %bitcast.33), channel_id=1, source_target_pairs={{0,4},{4,8},{8,12},{12,0},{1,5},{5,9},{9,13},{13,1},{2,6},{6,10},{... | collective-permute-start | bytes 12582920 | tf_op jit(solution)/shard_map/ppermute | solution.py:15
  127.2 2.0 copy-start.5
  129.1 92.6 %collective-permute-start.1 = (bf16[256,8192]{0,1:T(8,128)(2,1)S(1)}, bf16[256,8192]{0,1:T(8,128)(2,1)S(1)}, u32[]{:S(2)}, u32[]{:S(2)}) collective-permute-start(bf16[256,8192]{0,1:T(8,128)(2,1)S(1)} %collective-permute-done), channel_id=1, source_target_pairs={{0,4},{4,8},{8,12},{12,0},{1,5},{5,9},{9,13},{13,1},{2,6},{6,10},{... | collective-permute-start | bytes 12582920 | tf_op jit(solution)/shard_map/ppermute | solution.py:15
  221.8 2.0 copy-start.6
  223.7 91.8 %collective-permute-start.2 = (bf16[256,8192]{0,1:T(8,128)(2,1)S(1)}, bf16[256,8192]{0,1:T(8,128)(2,1)}, u32[]{:S(2)}, u32[]{:S(2)}) collective-permute-start(bf16[256,8192]{0,1:T(8,128)(2,1)S(1)} %collective-permute-done.1), channel_id=1, source_target_pairs={{0,4},{4,8},{8,12},{12,0},{1,5},{5,9},{9,13},{13,1},{2,6},{6,10},{... | collective-permute-start | bytes 12582920 | tf_op jit(solution)/shard_map/ppermute | solution.py:15
Sparse Core Ops, SparseCore 0:
  323.8 20.0 reduce-scatter.1
where the time goes:
time: 354 us; the launch traced here: 353 us
  waiting for transfers between devices  297 us (84%)
  matrix products  25.7 us (7%)
  local copies, waits for them, and re-layouts  13.9 us (4%)
  between operations  13.5 us (4%)
    ppermute x3, waiting for transfers between devices, shifted(): return lax.ppermute(value, axis, pairs)  277 us
    reduce_scatter x1, waiting for transfers between devices, local(): lax.psum_scatter(partial_value, 'feat', scatter_dimension=0, tiled=True)  20.2 us
    unnamed x21, local copies, waits for them, and re-layouts  12.4 us
    dot_general x1, matrix products, against(): lax.dot_general(query_rows, grads, (((1,), (1,)), ((), ())), preferred_el...  8.11 us
  transfers between devices with their start and end apart: 4, of which 4 were waited for; matrix products, arithmetic and copies ran while one was open for 0% of the time, Pallas kernels for 0%

commit v1 on v0

--- a/solution.py
+++ b/solution.py
@@ -1,12 +1,18 @@
+import functools
+
 import jax
 import jax.numpy as jnp
 from jax import lax
+from jax.experimental import pallas as pl
+from jax.experimental.pallas import tpu as pltpu
 from jax.sharding import PartitionSpec as P
 
 STEPS = 3
 
 
 DAMPING = 0.1
+
+MESH = pl.DeviceIdType.MESH
 
 
 def shifted(value, axis, steps):
@@ -60,19 +66,244 @@
     )
 
 
-def local(queries, grads, example_ids, layer_of_block, rot_out, rot_in, eig_out, eig_in):
+def ring_local(queries, grads, example_ids, layer_of_block, rot_out, rot_in, eig_out, eig_in):
     out_basis, in_basis, inverse = select_tables(layer_of_block, rot_out, rot_in, eig_out, eig_in)
     ready = precondition(queries, out_basis, in_basis, inverse)
-    received = [ready]
-    current = ready
-    for offset in range(STEPS):
-        current = shifted(current, "ex", 1)
-        received.append(current)
-    stacked = jnp.concatenate(received, axis=0)
-    partial_value = against(stacked, grads)
+    current = grads
+    pieces = []
+    for offset in range(STEPS + 1):
+        part = against(ready, current)
+        pieces.append(shifted(part, "ex", offset) if offset else part)
+        if offset < STEPS:
+            current = shifted(current, "ex", -1)
+    partial_value = jnp.concatenate(pieces, axis=0)
     owned_rows = lax.psum_scatter(partial_value, "feat", scatter_dimension=0, tiled=True)
-    example_major = owned_rows.T
-    return jnp.take(example_major, example_ids[0], axis=0)
+    return jnp.take(owned_rows.T, example_ids[0], axis=0)
+
+
+def dot_nt(a, b):
+    return lax.dot_general(a, b, (((1,), (1,)), ((), ())), preferred_element_type=jnp.float32)
+
+
+def dot_nn(a, b, precision=None):
+    return jnp.dot(a, b, preferred_element_type=jnp.float32, precision=precision)
+
+
+def line_kernel(
+    n, kout, kin, cols,
+    layer_ref, ids_ref, rot_out_ref, rot_in_ref, eig_out_ref, eig_in_ref, q_hbm, g_hbm,
+    out_ref,
+    q_buf, ready, x2, basis, u_rows, v_block, g_buf, slots, acc, parts,
+    q_sem, g_sem, send_sem, recv_sem, part_send, part_recv,
+):
+    j = lax.axis_index("ex")
+    f = lax.axis_index("feat")
+    blocks = ready.shape[0]
+    width = kout * kin
+    examples = g_buf.shape[1]
+
+    def at(ex, feat):
+        return {"ex": ex, "feat": feat}
+
+    def hbm_block(ref, b):
+        return ref.at[:, pl.ds(pl.multiple_of(b * width, width), width)]
+
+    def load_q(b):
+        return pltpu.make_async_copy(hbm_block(q_hbm, b), q_buf.at[b], q_sem.at[b])
+
+    def load_g(b):
+        return pltpu.make_async_copy(hbm_block(g_hbm, b), g_buf.at[b], g_sem.at[b])
+
+    def hop(d, r, b):
+        src = hbm_block(g_hbm, b) if r == 0 else slots.at[d, r - 1, b]
+        to = jnp.maximum(j - 1, 0) if d == 0 else jnp.minimum(j + 1, n - 1)
+        return pltpu.make_async_remote_copy(
+            src_ref=src, dst_ref=slots.at[d, r, b],
+            send_sem=send_sem.at[d, r, b], recv_sem=recv_sem.at[d, r, b],
+            device_id=at(to, f), device_id_type=MESH,
+        )
+
+    def sends(d, r):
+        if d == 0:
+            return jnp.logical_and(j > 0, j + r <= n - 1)
+        return jnp.logical_and(j < n - 1, j - r >= 0)
+
+    def receives(d, r):
+        if d == 0:
+            return j + 1 + r <= n - 1
+        return j - 1 - r >= 0
+
+    def send_part(s):
+        return pltpu.make_async_remote_copy(
+            src_ref=acc.at[s], dst_ref=parts.at[f],
+            send_sem=part_send.at[s], recv_sem=part_recv.at[f],
+            device_id=at(lax.rem(j + s, n), s), device_id_type=MESH,
+        )
+
+    for b in range(blocks):
+        load_q(b).start()
+        load_g(b).start()
+
+    barrier = pltpu.get_barrier_semaphore()
+    for e in range(n):
+        for h in range(cols):
+            @pl.when(jnp.logical_or(e != j, h != f))
+            def _():
+                pl.semaphore_signal(barrier, inc=1, device_id=at(e, h), device_id_type=MESH)
+    pl.semaphore_wait(barrier, n * cols - 1)
+
+    for b in range(blocks):
+        for d in range(2):
+            @pl.when(sends(d, 0))
+            def _(d=d, b=b):
+                hop(d, 0, b).start()
+
+    acc[...] = jnp.zeros_like(acc)
+
+    lane = lax.broadcasted_iota(jnp.int32, (kout, width), 1)
+    row = lax.broadcasted_iota(jnp.int32, (kout, width), 0)
+    spread_out = (lane // kin == row).astype(jnp.float32)
+    spread_in = (lane % kin == row).astype(jnp.float32)
+    group = v_block.shape[0]
+    reps = group // kin
+    lane_group = lax.broadcasted_iota(jnp.int32, (kin, group), 1) // kin
+    spread_group = spread_in[:, :group]
+    exact = lax.Precision.HIGHEST
+
+    def prepare(b):
+        layer = layer_ref[b]
+        u = rot_out_ref[layer]
+        v = rot_in_ref[layer]
+        u_rows[...] = dot_nn(u, spread_out.astype(jnp.bfloat16))
+        for p in range(kout):
+            basis[p * kin:(p + 1) * kin, :] = (u_rows[p:p + 1, :] * spread_in).astype(jnp.bfloat16)
+        v_wide = dot_nn(v, spread_group.astype(jnp.bfloat16))
+        for o in range(reps):
+            v_block[o * kin:(o + 1) * kin, :] = jnp.where(lane_group == o, v_wide, 0.0).astype(jnp.bfloat16)
+        eo = jnp.broadcast_to(eig_out_ref[pl.ds(layer, 1), :], (8, kout))
+        ei = jnp.broadcast_to(eig_in_ref[pl.ds(layer, 1), :], (8, kin))
+        inverse = 1.0 / (dot_nn(eo, spread_out, exact) * dot_nn(ei, spread_in, exact) + DAMPING)
+        inverse = inverse[0:1, :]
+        for c in range(width // group):
+            here = slice(c * group, (c + 1) * group)
+            first = dot_nn(q_buf[b], basis[:, here]).astype(jnp.bfloat16)
+            x2[:, here] = (dot_nn(first, v_block[...]) * inverse[:, here]).astype(jnp.bfloat16)
+        for c in range(width // group):
+            here = slice(c * group, (c + 1) * group)
+            third = dot_nt(x2[...], basis[here, :]).astype(jnp.bfloat16)
+            ready[b, :, here] = dot_nt(third, v_block[...]).astype(jnp.bfloat16)
+
+    def own(b, _):
+        load_q(b).wait()
+        load_g(b).wait()
+        prepare(b)
+        acc[0] += dot_nt(g_buf[b], ready[b])
+        return 0
+
+    lax.fori_loop(0, blocks, own, 0)
+
+    @pl.when(f == 0)
+    def _():
+        parts[0] = acc[0]
+
+    @pl.when(f != 0)
+    def _():
+        send_part(0).start()
+
+    for r in range(n - 1):
+        def step(b, _):
+            for d in range(2):
+                @pl.when(receives(d, r))
+                def _(d=d):
+                    hop(d, r, b).wait_recv()
+                if r + 1 < n - 1:
+                    @pl.when(sends(d, r + 1))
+                    def _(d=d):
+                        hop(d, r + 1, b).start()
+            for d in range(2):
+                s = r + 1 if d == 0 else n - 1 - r
+                @pl.when(receives(d, r))
+                def _(d=d, s=s):
+                    acc[s] += dot_nt(slots[d, r, b], ready[b])
+            return 0
+
+        lax.fori_loop(0, blocks, step, 0)
+        for d in range(2):
+            s = r + 1 if d == 0 else n - 1 - r
+            @pl.when(receives(d, r))
+            def _(s=s):
+                send_part(s).start()
+
+    for h in range(cols):
+        @pl.when(jnp.logical_not(jnp.logical_and(f == 0, h == 0)))
+        def _(h=h):
+            pltpu.make_async_remote_copy(
+                src_ref=acc.at[0], dst_ref=parts.at[h],
+                send_sem=part_send.at[0], recv_sem=part_recv.at[h],
+                device_id=at(j, f), device_id_type=MESH,
+            ).wait_recv()
+    acc_sum = parts[0]
+    for h in range(1, cols):
+        acc_sum += parts[h]
+    parts[0] = acc_sum
+    for r in range(examples):
+        out_ref[r:r + 1, :] = parts[0, pl.ds(ids_ref[0, r], 1), :]
+
+    @pl.when(f != 0)
+    def _():
+        send_part(0).wait_send()
+    for s in range(1, n):
+        send_part(s).wait_send()
+
+    for r in range(n - 1):
+        def drain(b, _):
+            for d in range(2):
+                @pl.when(sends(d, r))
+                def _(d=d):
+                    hop(d, r, b).wait_send()
+            return 0
+
+        lax.fori_loop(0, blocks, drain, 0)
+
+
+def line_local(n, cols, queries, grads, example_ids, layer_of_block, rot_out, rot_in, eig_out, eig_in):
+    rows = queries.shape[0]
+    examples = grads.shape[0]
+    blocks = layer_of_block.shape[0]
+    kout, kin = rot_out.shape[1], rot_in.shape[1]
+    width = kout * kin
+    group = min(256, width)
+    bf16, f32 = jnp.bfloat16, jnp.float32
+    smem = pl.BlockSpec(memory_space=pltpu.SMEM)
+    vmem = pl.BlockSpec(memory_space=pltpu.VMEM)
+    hbm = pl.BlockSpec(memory_space=pl.ANY)
+    return pl.pallas_call(
+        functools.partial(line_kernel, n, kout, kin, cols),
+        out_shape=jax.ShapeDtypeStruct((examples, rows), f32),
+        in_specs=[smem, smem, vmem, vmem, vmem, vmem, hbm, hbm],
+        out_specs=vmem,
+        scratch_shapes=[
+            pltpu.VMEM((blocks, rows, width), bf16),
+            pltpu.VMEM((blocks, rows, width), bf16),
+            pltpu.VMEM((rows, width), bf16),
+            pltpu.VMEM((width, width), bf16),
+            pltpu.VMEM((kout, width), f32),
+            pltpu.VMEM((group, group), bf16),
+            pltpu.VMEM((blocks, examples, width), bf16),
+            pltpu.VMEM((2, n - 1, blocks, examples, width), bf16),
+            pltpu.VMEM((n, examples, rows), f32),
+            pltpu.VMEM((cols, examples, rows), f32),
+            pltpu.SemaphoreType.DMA((blocks,)),
+            pltpu.SemaphoreType.DMA((blocks,)),
+            pltpu.SemaphoreType.DMA((2, n - 1, blocks)),
+            pltpu.SemaphoreType.DMA((2, n - 1, blocks)),
+            pltpu.SemaphoreType.DMA((n,)),
+            pltpu.SemaphoreType.DMA((cols,)),
+        ],
+        compiler_params=pltpu.CompilerParams(
+            collective_id=0, has_side_effects=True, vmem_limit_bytes=40 * 1024 * 1024
+        ),
+    )(layer_of_block, example_ids, rot_out, rot_in, eig_out, eig_in, queries, grads)
 
 
 def solution(mesh):
@@ -87,4 +318,6 @@
         P(),
     )
     out_specs = P(("grp", "ex"), "feat")
+    n, cols = mesh.shape["ex"], mesh.shape["feat"]
+    local = functools.partial(line_local, n, cols) if n == cols == STEPS + 1 else ring_local
     return jax.shard_map(local, mesh=mesh, in_specs=in_specs, out_specs=out_specs, check_vma=False)

time: 354 us -> 101 us (0.29)
  waiting for transfers between devices: 297 us -> 0 us
  Pallas kernels: 0 us -> 89.9 us
  matrix products: 25.7 us -> 0 us
  between operations: 13.5 us -> 0.04 us
    ppermute x3 -> x0, waiting for transfers between devices: 277 us -> none  [shifted(): return lax.ppermute(value, axis, pairs)]
    pallas_call x0 -> x1, Pallas kernels: none -> 89.9 us  [line_local(): pl.pallas_call(functools.partial(line_kernel, n, kout, kin, cols), out_sh...]
    dot_general x9 -> x0, matrix products: 25.7 us -> none  [the longest x1 8.11 us: against(): lax.dot_general(query_rows, grads, (((1,), (1,)), ((), ())), preferred_el...]
    reduce_scatter x1 -> x0, waiting for transfers between devices: 20.2 us -> none  [local(): lax.psum_scatter(partial_value, 'feat', scatter_dimension=0, tiled=True)]
    unnamed x21 -> x13, local copies, waits for them, and re-layouts: 12.4 us -> 10.7 us
  transfers between devices with their start and end apart: 4 -> 0, of which waited for: 4 -> 0; matrix products, arithmetic and copies ran while one was open for 0% -> 0% of each run, Pallas kernels for 0% -> 0%
where the time goes in v1:
time: 101 us
  Pallas kernels  89.9 us (89%)
  local copies, waits for them, and re-layouts  10.7 us (11%)
    pallas_call x1, Pallas kernels, line_local(): pl.pallas_call(functools.partial(line_kernel, n, kout, kin, cols), out_sh...  89.9 us
    unnamed x13, local copies, waits for them, and re-layouts  10.7 us

profile of v1, /device:TPU:1, one launch (start us, length us, event | category | flops | bytes accessed | tf_op | source)
XLA Modules:
  0.0 100.6 jit_solution(7171237272264010988)
XLA Ops:
  0.0 0.8 copy.11.eig_out_ref
  0.8 0.8 copy.12.eig_in_ref
  1.6 1.9 %copy.9.rot_out_ref = bf16[80,32,32]{2,1,0:T(8,128)(2,1)S(1)} copy(bf16[80,32,32]{0,2,1:T(8,128)(2,1)} %param.12) | data formatting | bytes 327680 | tf_op args[4]
  3.5 1.9 %copy.10.rot_in_ref = bf16[80,32,32]{2,1,0:T(8,128)(2,1)S(1)} copy(bf16[80,32,32]{0,2,1:T(8,128)(2,1)} %param.13) | data formatting | bytes 327680 | tf_op args[5]
  5.4 0.0 copy-start
  5.4 2.2 %copy-done = bf16[256,8192]{1,0:T(8,128)(2,1)S(1)} copy-done((bf16[256,8192]{1,0:T(8,128)(2,1)S(1)}, bf16[256,8192]{1,0:T(8,128)(2,1)}, u32[]{:S(2)}) %copy-start) | copy-done | bytes 4194328
  7.6 0.0 copy-start.1
  7.6 1.2 %copy-done.1 = bf16[64,8192]{1,0:T(8,128)(2,1)S(1)} copy-done((bf16[64,8192]{1,0:T(8,128)(2,1)S(1)}, bf16[64,8192]{1,0:T(8,128)(2,1)}, u32[]{:S(2)}) %copy-start.1) | copy-done | bytes 1048600
  8.8 0.0 copy-start.2
  8.8 0.7 copy-done.2
  9.5 0.0 copy-start.3
  9.5 0.7 copy-done.3
  10.1 89.9 %shard_map.82 = f32[64,256]{1,0:T(8,128)S(1)} custom-call(s32[8]{0:T(128)S(1)} %copy-done.2, s32[1,64]{1,0:T(1,128)S(1)} %copy-done.3, bf16[80,32,32]{2,1,0:T(8,128)(2,1)S(1)} %copy.9.rot_out_ref, bf16[80,32,32]{2,1,0:T(8,128)(2,1)S(1)} %copy.10.rot_in_ref, f32[80,32]{1,0:T(8,128)S(1)} %copy.11.eig_out_ref, f32[80,32]{1,0:T(8,128)S(1)} %copy.12.eig_in_ref, ...), custom_call_target="tpu_custom_call" | custom-call | tf_op jit(solution)/shard_map/pallas_call | solution.py:280
  100.0 0.6 copy.14
Async XLA Ops:
  5.4 2.2 %copy-start = (bf16[256,8192]{1,0:T(8,128)(2,1)S(1)}, bf16[256,8192]{1,0:T(8,128)(2,1)}, u32[]{:S(2)}) copy-start(bf16[256,8192]{1,0:T(8,128)(2,1)} %q_hbm.1) | copy-start | bytes 12582916
  7.6 1.2 %copy-start.1 = (bf16[64,8192]{1,0:T(8,128)(2,1)S(1)}, bf16[64,8192]{1,0:T(8,128)(2,1)}, u32[]{:S(2)}) copy-start(bf16[64,8192]{1,0:T(8,128)(2,1)} %g_hbm.1) | copy-start | bytes 3145732
  8.8 0.7 copy-start.2
  9.5 0.7 copy-start.3

commit v2 on v1

--- a/solution.py
+++ b/solution.py
@@ -90,23 +90,32 @@
 
 
 def line_kernel(
-    n, kout, kin, cols,
-    layer_ref, ids_ref, rot_out_ref, rot_in_ref, eig_out_ref, eig_in_ref, q_hbm, g_hbm,
+    n, kout, kin, cols, keep,
+    layer_ref, ids_ref, rot_out_hbm, rot_in_hbm, eig_out_hbm, eig_in_hbm, q_hbm, g_hbm,
     out_ref,
+    rot_out_t, rot_in_t, eig_out_t, eig_in_t, u_tab, v_tab, inv_tab,
     q_buf, ready, x2, basis, u_rows, v_block, g_buf, slots, acc, parts,
-    q_sem, g_sem, send_sem, recv_sem, part_send, part_recv,
+    far_q, far_ready, far_acc, far_parts,
+    table_sem, q_sem, g_sem, send_sem, recv_sem, part_send, part_recv,
+    far_send, far_recv, far_part_send, far_part_recv,
 ):
     j = lax.axis_index("ex")
     f = lax.axis_index("feat")
     blocks = ready.shape[0]
     width = kout * kin
     examples = g_buf.shape[1]
+    layers = rot_out_t.shape[1]
+    exact = lax.Precision.HIGHEST
 
     def at(ex, feat):
         return {"ex": ex, "feat": feat}
 
     def hbm_block(ref, b):
-        return ref.at[:, pl.ds(pl.multiple_of(b * width, width), width)]
+        if not isinstance(b, int):
+            b = pl.multiple_of(b * width, width)
+        else:
+            b = b * width
+        return ref.at[:, pl.ds(b, width)]
 
     def load_q(b):
         return pltpu.make_async_copy(hbm_block(q_hbm, b), q_buf.at[b], q_sem.at[b])
@@ -123,15 +132,28 @@
             device_id=at(to, f), device_id_type=MESH,
         )
 
-    def sends(d, r):
+    def sends(d, r, b):
         if d == 0:
-            return jnp.logical_and(j > 0, j + r <= n - 1)
-        return jnp.logical_and(j < n - 1, j - r >= 0)
-
-    def receives(d, r):
+            there = jnp.logical_and(j > 0, j + r <= n - 1)
+            return jnp.logical_and(there, jnp.logical_or(j != 1, b < keep))
+        there = jnp.logical_and(j < n - 1, j - r >= 0)
+        return jnp.logical_and(there, jnp.logical_or(j != n - 2, b < keep))
+
+    def receives(d, r, b):
         if d == 0:
-            return j + 1 + r <= n - 1
-        return j - 1 - r >= 0
+            return jnp.logical_and(j + 1 + r <= n - 1, jnp.logical_or(j != 0, b < keep))
+        return jnp.logical_and(j - 1 - r >= 0, jnp.logical_or(j != n - 1, b < keep))
+
+    def far(m):
+        return pltpu.make_async_remote_copy(
+            src_ref=hbm_block(q_hbm, keep + m), dst_ref=far_q.at[m],
+            send_sem=far_send.at[m], recv_sem=far_recv.at[m],
+            device_id=at(jnp.where(j < 2, 1, n - 2), f), device_id_type=MESH,
+        )
+
+    is_end = jnp.logical_or(j == 0, j == n - 1)
+    is_helper = jnp.logical_or(j == 1, j == n - 2)
+    low = j == 1
 
     def send_part(s):
         return pltpu.make_async_remote_copy(
@@ -140,9 +162,23 @@
             device_id=at(lax.rem(j + s, n), s), device_id_type=MESH,
         )
 
-    for b in range(blocks):
-        load_q(b).start()
-        load_g(b).start()
+    def far_feat(t):
+        return jnp.where(low, 1 + t, n - 1 - t)
+
+    def send_far_part(t):
+        return pltpu.make_async_remote_copy(
+            src_ref=far_acc.at[t], dst_ref=far_parts.at[f],
+            send_sem=far_part_send.at[t], recv_sem=far_part_recv.at[f],
+            device_id=at(jnp.where(low, 1 + t, n - 2 - t), far_feat(t)), device_id_type=MESH,
+        )
+
+    tables = [
+        pltpu.make_async_copy(src, dst, table_sem.at[i])
+        for i, (src, dst) in enumerate([
+            (rot_out_hbm, rot_out_t), (rot_in_hbm, rot_in_t),
+            (eig_out_hbm, eig_out_t), (eig_in_hbm, eig_in_t),
+        ])
+    ]
 
     barrier = pltpu.get_barrier_semaphore()
     for e in range(n):
@@ -150,15 +186,26 @@
             @pl.when(jnp.logical_or(e != j, h != f))
             def _():
                 pl.semaphore_signal(barrier, inc=1, device_id=at(e, h), device_id_type=MESH)
+    for table in tables:
+        table.start()
+    for b in range(blocks):
+        load_q(b).start()
+        load_g(b).start()
     pl.semaphore_wait(barrier, n * cols - 1)
 
+    moved = blocks - keep
     for b in range(blocks):
         for d in range(2):
-            @pl.when(sends(d, 0))
+            @pl.when(sends(d, 0, b))
             def _(d=d, b=b):
                 hop(d, 0, b).start()
+        if (b + 1) * moved % blocks == 0:
+            @pl.when(is_end)
+            def _(m=(b + 1) * moved // blocks - 1):
+                far(m).start()
 
     acc[...] = jnp.zeros_like(acc)
+    far_acc[...] = jnp.zeros_like(far_acc)
 
     lane = lax.broadcasted_iota(jnp.int32, (kout, width), 1)
     row = lax.broadcasted_iota(jnp.int32, (kout, width), 0)
@@ -168,38 +215,83 @@
     reps = group // kin
     lane_group = lax.broadcasted_iota(jnp.int32, (kin, group), 1) // kin
     spread_group = spread_in[:, :group]
-    exact = lax.Precision.HIGHEST
-
-    def prepare(b):
-        layer = layer_ref[b]
-        u = rot_out_ref[layer]
-        v = rot_in_ref[layer]
-        u_rows[...] = dot_nn(u, spread_out.astype(jnp.bfloat16))
+
+    level = lax.broadcasted_iota(jnp.int32, (blocks, layers), 1)
+    which = lax.broadcasted_iota(jnp.int32, (blocks, layers), 0)
+    onehot = jnp.zeros((blocks, layers), jnp.float32)
+    for b in range(blocks):
+        onehot = jnp.where(jnp.logical_and(which == b, level == layer_ref[b]), 1.0, onehot)
+    for table in tables:
+        table.wait()
+    for ref, tab, rows in ((rot_out_t, u_tab, kout), (rot_in_t, v_tab, kin)):
+        flat = dot_nt(onehot.astype(jnp.bfloat16), ref[...])
+        for p in range(rows):
+            piece = flat[:, p * rows:(p + 1) * rows]
+            for b in range(blocks):
+                tab[b, p:p + 1, :] = piece[b:b + 1, :]
+    dot_nt_exact = functools.partial(
+        lax.dot_general, dimension_numbers=(((1,), (1,)), ((), ())),
+        precision=exact, preferred_element_type=jnp.float32,
+    )
+    eo = dot_nt_exact(onehot, eig_out_t[...])
+    ei = dot_nt_exact(onehot, eig_in_t[...])
+    inv_tab[...] = 1.0 / (dot_nn(eo, spread_out, exact) * dot_nn(ei, spread_in, exact) + DAMPING)
+
+    def prepare(b, src, dst, slot):
+        u_rows[...] = dot_nn(u_tab[b].astype(jnp.bfloat16), spread_out.astype(jnp.bfloat16))
         for p in range(kout):
             basis[p * kin:(p + 1) * kin, :] = (u_rows[p:p + 1, :] * spread_in).astype(jnp.bfloat16)
-        v_wide = dot_nn(v, spread_group.astype(jnp.bfloat16))
+        v_wide = dot_nn(v_tab[b].astype(jnp.bfloat16), spread_group.astype(jnp.bfloat16))
         for o in range(reps):
             v_block[o * kin:(o + 1) * kin, :] = jnp.where(lane_group == o, v_wide, 0.0).astype(jnp.bfloat16)
-        eo = jnp.broadcast_to(eig_out_ref[pl.ds(layer, 1), :], (8, kout))
-        ei = jnp.broadcast_to(eig_in_ref[pl.ds(layer, 1), :], (8, kin))
-        inverse = 1.0 / (dot_nn(eo, spread_out, exact) * dot_nn(ei, spread_in, exact) + DAMPING)
-        inverse = inverse[0:1, :]
+        inverse = inv_tab[pl.ds(b, 1), :]
         for c in range(width // group):
             here = slice(c * group, (c + 1) * group)
-            first = dot_nn(q_buf[b], basis[:, here]).astype(jnp.bfloat16)
+            first = dot_nn(src[slot], basis[:, here]).astype(jnp.bfloat16)
             x2[:, here] = (dot_nn(first, v_block[...]) * inverse[:, here]).astype(jnp.bfloat16)
         for c in range(width // group):
             here = slice(c * group, (c + 1) * group)
             third = dot_nt(x2[...], basis[here, :]).astype(jnp.bfloat16)
-            ready[b, :, here] = dot_nt(third, v_block[...]).astype(jnp.bfloat16)
+            dst[slot, :, here] = dot_nt(third, v_block[...]).astype(jnp.bfloat16)
+
+    def step(r, b):
+        for d in range(2):
+            @pl.when(receives(d, r, b))
+            def _(d=d):
+                hop(d, r, b).wait_recv()
+            if r + 1 < n - 1:
+                @pl.when(sends(d, r + 1, b))
+                def _(d=d):
+                    hop(d, r + 1, b).start()
+        for d in range(2):
+            s = r + 1 if d == 0 else n - 1 - r
+            @pl.when(receives(d, r, b))
+            def _(d=d, s=s):
+                acc[s] += dot_nt(slots[d, r, b], ready[b])
+
+    def finish(r):
+        for d in range(2):
+            s = r + 1 if d == 0 else n - 1 - r
+            @pl.when(receives(d, r, 0))
+            def _(s=s):
+                send_part(s).start()
 
     def own(b, _):
         load_q(b).wait()
         load_g(b).wait()
-        prepare(b)
+        prepare(b, q_buf, ready, b)
         acc[0] += dot_nt(g_buf[b], ready[b])
+        step(0, b)
         return 0
 
+    def later(r):
+        def body(b, _):
+            step(r, b)
+            return 0
+
+        lax.fori_loop(0, blocks, body, 0)
+        finish(r)
+
     lax.fori_loop(0, blocks, own, 0)
 
     @pl.when(f == 0)
@@ -210,42 +302,72 @@
     def _():
         send_part(0).start()
 
-    for r in range(n - 1):
-        def step(b, _):
-            for d in range(2):
-                @pl.when(receives(d, r))
-                def _(d=d):
-                    hop(d, r, b).wait_recv()
-                if r + 1 < n - 1:
-                    @pl.when(sends(d, r + 1))
-                    def _(d=d):
-                        hop(d, r + 1, b).start()
-            for d in range(2):
-                s = r + 1 if d == 0 else n - 1 - r
-                @pl.when(receives(d, r))
-                def _(d=d, s=s):
-                    acc[s] += dot_nt(slots[d, r, b], ready[b])
-            return 0
-
-        lax.fori_loop(0, blocks, step, 0)
-        for d in range(2):
-            s = r + 1 if d == 0 else n - 1 - r
-            @pl.when(receives(d, r))
-            def _(s=s):
-                send_part(s).start()
+    finish(0)
+
+    def help_out(m):
+        @pl.when(is_helper)
+        def _():
+            far(m).wait_recv()
+            prepare(keep + m, far_q, far_ready, m)
+
+    half = moved // 2
+    for m in range(half):
+        help_out(m)
+    later(1)
+    for m in range(half, moved):
+        help_out(m)
+
+    @pl.when(is_helper)
+    def _():
+        side = jnp.where(low, 0, 1)
+        for m in range(moved):
+            far_acc[0] += dot_nt(g_buf[keep + m], far_ready[m])
+            for r in range(n - 2):
+                far_acc[1 + r] += dot_nt(slots[side, r, keep + m], far_ready[m])
+
+    for t in range(n - 1):
+        here = jnp.logical_and(t == 0, far_feat(t) == f)
+
+        @pl.when(jnp.logical_and(is_helper, here))
+        def _(t=t):
+            far_parts[pl.ds(f, 1)] = far_acc[t:t + 1]
+
+        @pl.when(jnp.logical_and(is_helper, jnp.logical_not(here)))
+        def _(t=t):
+            send_far_part(t).start()
+
+    later(2)
+
+    def arrived(ref, sem, h):
+        return pltpu.make_async_remote_copy(
+            src_ref=acc.at[0], dst_ref=ref.at[h],
+            send_sem=part_send.at[0], recv_sem=sem.at[h],
+            device_id=at(j, f), device_id_type=MESH,
+        )
+
+    k = lax.rem(j - f + n, n)
+    split = jnp.logical_and(f != 0, jnp.logical_or(k == 0, k == n - 1))
+    helper_of = jnp.where(k == 0, 1, n - 2)
+
+    @pl.when(split)
+    def _():
+        for h in range(cols):
+            @pl.when(jnp.logical_or(helper_of != j, h != f))
+            def _(h=h):
+                arrived(far_parts, far_part_recv, h).wait_recv()
+        total = far_parts[0]
+        for h in range(1, cols):
+            total += far_parts[h]
+        far_acc[n - 1] = total
 
     for h in range(cols):
         @pl.when(jnp.logical_not(jnp.logical_and(f == 0, h == 0)))
         def _(h=h):
-            pltpu.make_async_remote_copy(
-                src_ref=acc.at[0], dst_ref=parts.at[h],
-                send_sem=part_send.at[0], recv_sem=part_recv.at[h],
-                device_id=at(j, f), device_id_type=MESH,
-            ).wait_recv()
-    acc_sum = parts[0]
+            arrived(parts, part_recv, h).wait_recv()
+    total = far_acc[n - 1] + parts[0]
     for h in range(1, cols):
-        acc_sum += parts[h]
-    parts[0] = acc_sum
+        total += parts[h]
+    parts[0] = total
     for r in range(examples):
         out_ref[r:r + 1, :] = parts[0, pl.ds(ids_ref[0, r], 1), :]
 
@@ -254,11 +376,22 @@
         send_part(0).wait_send()
     for s in range(1, n):
         send_part(s).wait_send()
+    for t in range(n - 1):
+        here = jnp.logical_and(t == 0, far_feat(t) == f)
+
+        @pl.when(jnp.logical_and(is_helper, jnp.logical_not(here)))
+        def _(t=t):
+            send_far_part(t).wait_send()
+
+    @pl.when(is_end)
+    def _():
+        for m in range(moved):
+            far(m).wait_send()
 
     for r in range(n - 1):
         def drain(b, _):
             for d in range(2):
-                @pl.when(sends(d, r))
+                @pl.when(sends(d, r, b))
                 def _(d=d):
                     hop(d, r, b).wait_send()
             return 0
@@ -270,19 +403,29 @@
     rows = queries.shape[0]
     examples = grads.shape[0]
     blocks = layer_of_block.shape[0]
-    kout, kin = rot_out.shape[1], rot_in.shape[1]
+    layers, kout, kin = rot_out.shape[0], rot_out.shape[1], rot_in.shape[1]
     width = kout * kin
     group = min(256, width)
+    keep = blocks - blocks // 4
+    moved = blocks - keep
     bf16, f32 = jnp.bfloat16, jnp.float32
     smem = pl.BlockSpec(memory_space=pltpu.SMEM)
     vmem = pl.BlockSpec(memory_space=pltpu.VMEM)
     hbm = pl.BlockSpec(memory_space=pl.ANY)
+    dma = pltpu.SemaphoreType.DMA
     return pl.pallas_call(
-        functools.partial(line_kernel, n, kout, kin, cols),
+        functools.partial(line_kernel, n, kout, kin, cols, keep),
         out_shape=jax.ShapeDtypeStruct((examples, rows), f32),
-        in_specs=[smem, smem, vmem, vmem, vmem, vmem, hbm, hbm],
+        in_specs=[smem, smem] + [hbm] * 6,
         out_specs=vmem,
         scratch_shapes=[
+            pltpu.VMEM((kout * kout, layers), bf16),
+            pltpu.VMEM((kin * kin, layers), bf16),
+            pltpu.VMEM((kout, layers), f32),
+            pltpu.VMEM((kin, layers), f32),
+            pltpu.VMEM((blocks, kout, kout), f32),
+            pltpu.VMEM((blocks, kin, kin), f32),
+            pltpu.VMEM((blocks, width), f32),
             pltpu.VMEM((blocks, rows, width), bf16),
             pltpu.VMEM((blocks, rows, width), bf16),
             pltpu.VMEM((rows, width), bf16),
@@ -293,17 +436,31 @@
             pltpu.VMEM((2, n - 1, blocks, examples, width), bf16),
             pltpu.VMEM((n, examples, rows), f32),
             pltpu.VMEM((cols, examples, rows), f32),
-            pltpu.SemaphoreType.DMA((blocks,)),
-            pltpu.SemaphoreType.DMA((blocks,)),
-            pltpu.SemaphoreType.DMA((2, n - 1, blocks)),
-            pltpu.SemaphoreType.DMA((2, n - 1, blocks)),
-            pltpu.SemaphoreType.DMA((n,)),
-            pltpu.SemaphoreType.DMA((cols,)),
+            pltpu.VMEM((moved, rows, width), bf16),
+            pltpu.VMEM((moved, rows, width), bf16),
+            pltpu.VMEM((n, examples, rows), f32),
+            pltpu.VMEM((cols, examples, rows), f32),
+            dma((4,)),
+            dma((blocks,)),
+            dma((blocks,)),
+            dma((2, n - 1, blocks)),
+            dma((2, n - 1, blocks)),
+            dma((n,)),
+            dma((cols,)),
+            dma((moved,)),
+            dma((moved,)),
+            dma((n - 1,)),
+            dma((cols,)),
         ],
         compiler_params=pltpu.CompilerParams(
-            collective_id=0, has_side_effects=True, vmem_limit_bytes=40 * 1024 * 1024
+            collective_id=0, has_side_effects=True, vmem_limit_bytes=58 * 1024 * 1024
         ),
-    )(layer_of_block, example_ids, rot_out, rot_in, eig_out, eig_in, queries, grads)
+    )(
+        layer_of_block, example_ids,
+        rot_out.transpose(1, 2, 0).reshape(kout * kout, layers),
+        rot_in.transpose(1, 2, 0).reshape(kin * kin, layers),
+        eig_out.T, eig_in.T, queries, grads,
+    )
 
 
 def solution(mesh):

time: 101 us -> 79 us (0.78)
  Pallas kernels: 89.9 us -> 77.3 us
  local copies, waits for them, and re-layouts: 10.7 us -> 1.47 us
    pallas_call x1, Pallas kernels: 89.9 us -> 77.3 us  [line_local(): pl.pallas_call(functools.partial(line_kernel, n, kout, kin, cols, keep),...]
    unnamed x13 -> x1, local copies, waits for them, and re-layouts: 10.7 us -> 1.47 us
where the time goes in v2:
time: 79 us; the launch traced here: 78.8 us
  Pallas kernels  77.3 us (98%)
  local copies, waits for them, and re-layouts  1.47 us (2%)
    pallas_call x1, Pallas kernels, line_local(): pl.pallas_call(functools.partial(line_kernel, n, kout, kin, cols, keep),...  77.3 us

profile of v2, /device:TPU:1, one launch (start us, length us, event | category | flops | bytes accessed | tf_op | source)
XLA Modules:
  0.0 78.8 jit_solution(16658851592471206940)
XLA Ops:
  0.0 77.3 %shard_map.82 = f32[64,256]{1,0:T(8,128)} custom-call(s32[8]{0:T(128)} %layer_ref.1, s32[1,64]{1,0:T(1,128)} %ids_ref.1, bf16[1024,80]{1,0:T(8,128)(2,1)} %bitcast.8, bf16[1024,80]{1,0:T(8,128)(2,1)} %bitcast.9, f32[32,80]{1,0:T(8,128)} %bitcast.10, f32[32,80]{1,0:T(8,128)} %bitcast.11, bf16[256,8192]{1,0:T(8,128)(2,1)} %q_hbm.1, bf16[64,8192]{1,0:T(8,128)(2,1)} %g_hbm.1), custom_call_target="tpu_custom_call" | custom-call | tf_op jit(solution)/shard_map/pallas_call | solution.py:416
  77.3 1.5 %copy.10 = f32[64,256]{1,0:T(8,128)} copy(f32[64,256]{1,0:T(8,128)} %shard_map.82) | data formatting | bytes 131072

commit v3 on v2

--- a/solution.py
+++ b/solution.py
@@ -90,12 +90,12 @@
 
 
 def line_kernel(
-    n, kout, kin, cols, keep,
+    n, kout, kin, cols, moved,
     layer_ref, ids_ref, rot_out_hbm, rot_in_hbm, eig_out_hbm, eig_in_hbm, q_hbm, g_hbm,
     out_ref,
     rot_out_t, rot_in_t, eig_out_t, eig_in_t, u_tab, v_tab, inv_tab,
     q_buf, ready, x2, basis, u_rows, v_block, g_buf, slots, acc, parts,
-    far_q, far_ready, far_acc, far_parts,
+    far_ready, far_acc, far_parts, packed, far_packed,
     table_sem, q_sem, g_sem, send_sem, recv_sem, part_send, part_recv,
     far_send, far_recv, far_part_send, far_part_recv,
 ):
@@ -135,18 +135,18 @@
     def sends(d, r, b):
         if d == 0:
             there = jnp.logical_and(j > 0, j + r <= n - 1)
-            return jnp.logical_and(there, jnp.logical_or(j != 1, b < keep))
+            return jnp.logical_and(there, jnp.logical_or(j != 1, b >= moved))
         there = jnp.logical_and(j < n - 1, j - r >= 0)
-        return jnp.logical_and(there, jnp.logical_or(j != n - 2, b < keep))
+        return jnp.logical_and(there, jnp.logical_or(j != n - 2, b >= moved))
 
     def receives(d, r, b):
         if d == 0:
-            return jnp.logical_and(j + 1 + r <= n - 1, jnp.logical_or(j != 0, b < keep))
-        return jnp.logical_and(j - 1 - r >= 0, jnp.logical_or(j != n - 1, b < keep))
+            return jnp.logical_and(j + 1 + r <= n - 1, jnp.logical_or(j != 0, b >= moved))
+        return jnp.logical_and(j - 1 - r >= 0, jnp.logical_or(j != n - 1, b >= moved))
 
     def far(m):
         return pltpu.make_async_remote_copy(
-            src_ref=hbm_block(q_hbm, keep + m), dst_ref=far_q.at[m],
+            src_ref=ready.at[m], dst_ref=far_ready.at[m],
             send_sem=far_send.at[m], recv_sem=far_recv.at[m],
             device_id=at(jnp.where(j < 2, 1, n - 2), f), device_id_type=MESH,
         )
@@ -157,7 +157,7 @@
 
     def send_part(s):
         return pltpu.make_async_remote_copy(
-            src_ref=acc.at[s], dst_ref=parts.at[f],
+            src_ref=packed.at[s], dst_ref=parts.at[f],
             send_sem=part_send.at[s], recv_sem=part_recv.at[f],
             device_id=at(lax.rem(j + s, n), s), device_id_type=MESH,
         )
@@ -167,7 +167,7 @@
 
     def send_far_part(t):
         return pltpu.make_async_remote_copy(
-            src_ref=far_acc.at[t], dst_ref=far_parts.at[f],
+            src_ref=far_packed.at[t], dst_ref=far_parts.at[f],
             send_sem=far_part_send.at[t], recv_sem=far_part_recv.at[f],
             device_id=at(jnp.where(low, 1 + t, n - 2 - t), far_feat(t)), device_id_type=MESH,
         )
@@ -193,16 +193,11 @@
         load_g(b).start()
     pl.semaphore_wait(barrier, n * cols - 1)
 
-    moved = blocks - keep
     for b in range(blocks):
         for d in range(2):
             @pl.when(sends(d, 0, b))
             def _(d=d, b=b):
                 hop(d, 0, b).start()
-        if (b + 1) * moved % blocks == 0:
-            @pl.when(is_end)
-            def _(m=(b + 1) * moved // blocks - 1):
-                far(m).start()
 
     acc[...] = jnp.zeros_like(acc)
     far_acc[...] = jnp.zeros_like(far_acc)
@@ -237,7 +232,7 @@
     ei = dot_nt_exact(onehot, eig_in_t[...])
     inv_tab[...] = 1.0 / (dot_nn(eo, spread_out, exact) * dot_nn(ei, spread_in, exact) + DAMPING)
 
-    def prepare(b, src, dst, slot):
+    def prepare(b):
         u_rows[...] = dot_nn(u_tab[b].astype(jnp.bfloat16), spread_out.astype(jnp.bfloat16))
         for p in range(kout):
             basis[p * kin:(p + 1) * kin, :] = (u_rows[p:p + 1, :] * spread_in).astype(jnp.bfloat16)
@@ -247,14 +242,14 @@
         inverse = inv_tab[pl.ds(b, 1), :]
         for c in range(width // group):
             here = slice(c * group, (c + 1) * group)
-            first = dot_nn(src[slot], basis[:, here]).astype(jnp.bfloat16)
+            first = dot_nn(q_buf[b], basis[:, here]).astype(jnp.bfloat16)
             x2[:, here] = (dot_nn(first, v_block[...]) * inverse[:, here]).astype(jnp.bfloat16)
         for c in range(width // group):
             here = slice(c * group, (c + 1) * group)
             third = dot_nt(x2[...], basis[here, :]).astype(jnp.bfloat16)
-            dst[slot, :, here] = dot_nt(third, v_block[...]).astype(jnp.bfloat16)
-
-    def step(r, b):
+            ready[b, :, here] = dot_nt(third, v_block[...]).astype(jnp.bfloat16)
+
+    def forward(r, b):
         for d in range(2):
             @pl.when(receives(d, r, b))
             def _(d=d):
@@ -263,6 +258,8 @@
                 @pl.when(sends(d, r + 1, b))
                 def _(d=d):
                     hop(d, r + 1, b).start()
+
+    def multiply(r, b):
         for d in range(2):
             s = r + 1 if d == 0 else n - 1 - r
             @pl.when(receives(d, r, b))
@@ -272,21 +269,40 @@
     def finish(r):
         for d in range(2):
             s = r + 1 if d == 0 else n - 1 - r
-            @pl.when(receives(d, r, 0))
+            @pl.when(receives(d, r, blocks - 1))
             def _(s=s):
+                packed[s] = acc[s].astype(packed.dtype)
                 send_part(s).start()
 
     def own(b, _):
         load_q(b).wait()
         load_g(b).wait()
-        prepare(b, q_buf, ready, b)
+        prepare(b)
+
+        @pl.when(jnp.logical_and(is_end, b < moved))
+        def _():
+            far(b).start()
+
+        forward(0, b)
         acc[0] += dot_nt(g_buf[b], ready[b])
-        step(0, b)
+        multiply(0, b)
+
+        @pl.when(b >= blocks - 2)
+        def _():
+            for i in range(2):
+                forward(1, (b - (blocks - 2)) * 2 + i)
+
         return 0
 
     def later(r):
         def body(b, _):
-            step(r, b)
+            if r == 1:
+                @pl.when(b >= 4)
+                def _():
+                    forward(r, b)
+            else:
+                forward(r, b)
+            multiply(r, b)
             return 0
 
         lax.fori_loop(0, blocks, body, 0)
@@ -296,51 +312,43 @@
 
     @pl.when(f == 0)
     def _():
-        parts[0] = acc[0]
+        parts[0] = acc[0].astype(parts.dtype)
 
     @pl.when(f != 0)
     def _():
+        packed[0] = acc[0].astype(packed.dtype)
         send_part(0).start()
 
     finish(0)
 
-    def help_out(m):
-        @pl.when(is_helper)
-        def _():
-            far(m).wait_recv()
-            prepare(keep + m, far_q, far_ready, m)
-
-    half = moved // 2
-    for m in range(half):
-        help_out(m)
     later(1)
-    for m in range(half, moved):
-        help_out(m)
 
     @pl.when(is_helper)
     def _():
         side = jnp.where(low, 0, 1)
         for m in range(moved):
-            far_acc[0] += dot_nt(g_buf[keep + m], far_ready[m])
+            far(m).wait_recv()
+            far_acc[0] += dot_nt(g_buf[m], far_ready[m])
             for r in range(n - 2):
-                far_acc[1 + r] += dot_nt(slots[side, r, keep + m], far_ready[m])
+                far_acc[1 + r] += dot_nt(slots[side, r, m], far_ready[m])
 
     for t in range(n - 1):
         here = jnp.logical_and(t == 0, far_feat(t) == f)
 
         @pl.when(jnp.logical_and(is_helper, here))
         def _(t=t):
-            far_parts[pl.ds(f, 1)] = far_acc[t:t + 1]
+            far_parts[pl.ds(f, 1)] = far_acc[t:t + 1].astype(far_parts.dtype)
 
         @pl.when(jnp.logical_and(is_helper, jnp.logical_not(here)))
         def _(t=t):
+            far_packed[t] = far_acc[t].astype(far_packed.dtype)
             send_far_part(t).start()
 
     later(2)
 
     def arrived(ref, sem, h):
         return pltpu.make_async_remote_copy(
-            src_ref=acc.at[0], dst_ref=ref.at[h],
+            src_ref=packed.at[0], dst_ref=ref.at[h],
             send_sem=part_send.at[0], recv_sem=sem.at[h],
             device_id=at(j, f), device_id_type=MESH,
         )
@@ -355,21 +363,21 @@
             @pl.when(jnp.logical_or(helper_of != j, h != f))
             def _(h=h):
                 arrived(far_parts, far_part_recv, h).wait_recv()
-        total = far_parts[0]
+        total = far_parts[0].astype(jnp.float32)
         for h in range(1, cols):
-            total += far_parts[h]
+            total += far_parts[h].astype(jnp.float32)
         far_acc[n - 1] = total
 
     for h in range(cols):
         @pl.when(jnp.logical_not(jnp.logical_and(f == 0, h == 0)))
         def _(h=h):
             arrived(parts, part_recv, h).wait_recv()
-    total = far_acc[n - 1] + parts[0]
+    total = far_acc[n - 1] + parts[0].astype(jnp.float32)
     for h in range(1, cols):
-        total += parts[h]
-    parts[0] = total
+        total += parts[h].astype(jnp.float32)
+    acc[0] = total
     for r in range(examples):
-        out_ref[r:r + 1, :] = parts[0, pl.ds(ids_ref[0, r], 1), :]
+        out_ref[r:r + 1, :] = acc[0, pl.ds(ids_ref[0, r], 1), :]
 
     @pl.when(f != 0)
     def _():
@@ -406,15 +414,14 @@
     layers, kout, kin = rot_out.shape[0], rot_out.shape[1], rot_in.shape[1]
     width = kout * kin
     group = min(256, width)
-    keep = blocks - blocks // 4
-    moved = blocks - keep
+    moved = blocks // 4
     bf16, f32 = jnp.bfloat16, jnp.float32
     smem = pl.BlockSpec(memory_space=pltpu.SMEM)
     vmem = pl.BlockSpec(memory_space=pltpu.VMEM)
     hbm = pl.BlockSpec(memory_space=pl.ANY)
     dma = pltpu.SemaphoreType.DMA
     return pl.pallas_call(
-        functools.partial(line_kernel, n, kout, kin, cols, keep),
+        functools.partial(line_kernel, n, kout, kin, cols, moved),
         out_shape=jax.ShapeDtypeStruct((examples, rows), f32),
         in_specs=[smem, smem] + [hbm] * 6,
         out_specs=vmem,
@@ -435,11 +442,12 @@
             pltpu.VMEM((blocks, examples, width), bf16),
             pltpu.VMEM((2, n - 1, blocks, examples, width), bf16),
             pltpu.VMEM((n, examples, rows), f32),
-            pltpu.VMEM((cols, examples, rows), f32),
-            pltpu.VMEM((moved, rows, width), bf16),
+            pltpu.VMEM((cols, examples, rows), bf16),
             pltpu.VMEM((moved, rows, width), bf16),
             pltpu.VMEM((n, examples, rows), f32),
-            pltpu.VMEM((cols, examples, rows), f32),
+            pltpu.VMEM((cols, examples, rows), bf16),
+            pltpu.VMEM((n, examples, rows), bf16),
+            pltpu.VMEM((n - 1, examples, rows), bf16),
             dma((4,)),
             dma((blocks,)),
             dma((blocks,)),

time: 79 us -> 72.2 us (0.914)
  Pallas kernels: 77.3 us -> 70.6 us
    pallas_call x1, Pallas kernels: 77.3 us -> 70.6 us  [line_local(): pl.pallas_call(functools.partial(line_kernel, n, kout, kin, cols, moved),...]
where the time goes in v3:
time: 72.2 us; the launch traced here: 72 us
  Pallas kernels  70.6 us (98%)
  local copies, waits for them, and re-layouts  1.47 us (2%)
    pallas_call x1, Pallas kernels, line_local(): pl.pallas_call(functools.partial(line_kernel, n, kout, kin, cols, moved),...  70.6 us
    unnamed x1, local copies, waits for them, and re-layouts  1.47 us

profile of v3, /device:TPU:1, one launch (start us, length us, event | category | flops | bytes accessed | tf_op | source)
XLA Modules:
  0.0 72.0 jit_solution(2507712163961300925)
XLA Ops:
  0.0 70.6 %shard_map.82 = f32[64,256]{1,0:T(8,128)} custom-call(s32[8]{0:T(128)} %layer_ref.1, s32[1,64]{1,0:T(1,128)} %ids_ref.1, bf16[1024,80]{1,0:T(8,128)(2,1)} %bitcast.8, bf16[1024,80]{1,0:T(8,128)(2,1)} %bitcast.9, f32[32,80]{1,0:T(8,128)} %bitcast.10, f32[32,80]{1,0:T(8,128)} %bitcast.11, bf16[256,8192]{1,0:T(8,128)(2,1)} %q_hbm.1, bf16[64,8192]{1,0:T(8,128)(2,1)} %g_hbm.1), custom_call_target="tpu_custom_call" | custom-call | tf_op jit(solution)/shard_map/pallas_call | solution.py:423
  70.6 1.5 %copy.10 = f32[64,256]{1,0:T(8,128)} copy(f32[64,256]{1,0:T(8,128)} %shard_map.82) | data formatting | bytes 131072

commit v4 on v3

--- a/solution.py
+++ b/solution.py
@@ -283,21 +283,20 @@
         def _():
             far(b).start()
 
-        forward(0, b)
+        for i in range(blocks):
+            @pl.when(b == i)
+            def _(i=i):
+                for c in range(i * 3 // 2, (i + 1) * 3 // 2):
+                    forward(c // blocks, c % blocks)
+
         acc[0] += dot_nt(g_buf[b], ready[b])
         multiply(0, b)
-
-        @pl.when(b >= blocks - 2)
-        def _():
-            for i in range(2):
-                forward(1, (b - (blocks - 2)) * 2 + i)
-
         return 0
 
     def later(r):
         def body(b, _):
             if r == 1:
-                @pl.when(b >= 4)
+                @pl.when(b >= blocks * 3 // 2 - blocks)
                 def _():
                     forward(r, b)
             else:

time: 72.2 us -> 71.3 us (0.988)
  Pallas kernels: 70.6 us -> 69.7 us
    pallas_call x1, Pallas kernels: 70.6 us -> 69.7 us  [line_local(): pl.pallas_call(functools.partial(line_kernel, n, kout, kin, cols, moved),...]
where the time goes in v4:
time: 71.3 us; the launch traced here: 71.2 us
  Pallas kernels  69.7 us (98%)
  local copies, waits for them, and re-layouts  1.47 us (2%)
    pallas_call x1, Pallas kernels, line_local(): pl.pallas_call(functools.partial(line_kernel, n, kout, kin, cols, moved),...  69.7 us
    unnamed x1, local copies, waits for them, and re-layouts  1.47 us

profile of v4, /device:TPU:1, one launch (start us, length us, event | category | flops | bytes accessed | tf_op | source)
XLA Modules:
  0.0 71.2 jit_solution(10572225217964300782)
XLA Ops:
  0.0 69.7 %shard_map.82 = f32[64,256]{1,0:T(8,128)} custom-call(s32[8]{0:T(128)} %layer_ref.1, s32[1,64]{1,0:T(1,128)} %ids_ref.1, bf16[1024,80]{1,0:T(8,128)(2,1)} %bitcast.8, bf16[1024,80]{1,0:T(8,128)(2,1)} %bitcast.9, f32[32,80]{1,0:T(8,128)} %bitcast.10, f32[32,80]{1,0:T(8,128)} %bitcast.11, bf16[256,8192]{1,0:T(8,128)(2,1)} %q_hbm.1, bf16[64,8192]{1,0:T(8,128)(2,1)} %g_hbm.1), custom_call_target="tpu_custom_call" | custom-call | tf_op jit(solution)/shard_map/pallas_call | solution.py:422
  69.7 1.5 %copy.10 = f32[64,256]{1,0:T(8,128)} copy(f32[64,256]{1,0:T(8,128)} %shard_map.82) | data formatting | bytes 131072
